TPU v7x, 32 devices: a whole 2x2x4 slice. The times are simulated.
32 devices in a mesh: row: 4 (over y, x), col: 8 (over z, core).
Axes of the slice: x: 2, y: 2, z: 4, core: 2. Of those that a mesh axis runs over, the one named last changes fastest.
Arguments:
- values: bfloat16 [4096, 4096], P('row', 'col'), may hold values from -1.5 to 1.5
- pattern: int32 [16, 16], P('row', 'col'), may hold values from 0 to 1, as said below
- sections: int32 [4], replicated, may hold values from 0 to 15
Outputs:
- exposure: bfloat16 [4096, 4096], P('row', 'col')
Inputs may be any that keep to these rules, and one draw needn't show every extreme that they name: `pattern`: 1 where a tile is stored, else 0; the share of stored tiles differs from tile row to tile row.
All inputs are finite; a program needn't handle non-finite values.
Results may differ from a plain program's by a relative error of at most 0.001.
Values may be sent and summed in bfloat16 or wider, within the bound.
No kernel may reach another device: no remote copies, remote signals or barrier semaphores. Data moves between devices by JAX's collectives and lax.ppermute only.
A program may use at most 64 MiB of HBM per device.

v0:
```python
import functools

import jax
import jax.numpy as jnp
from jax import lax
from jax.experimental import pallas as pl
from jax.experimental.pallas import tpu as pltpu
from jax.sharding import PartitionSpec as P

TILE = 256
SECTIONS = 4
CORES = 2
PARTS = 2
LAG = 2
PAIR = 2
STRIP = 128
BLOCKS = 2
STEPS_A_WORD = 8
BF16 = jnp.bfloat16
ANY = pl.BlockSpec(memory_space=pl.ANY)
SMEM = pl.BlockSpec(memory_space=pltpu.SMEM)
VMEM = pl.BlockSpec(memory_space=pltpu.VMEM)
HBM = pl.BlockSpec(memory_space=pltpu.HBM)
PARAMS = pltpu.CompilerParams(vmem_limit_bytes=32 * 1024 * 1024)


def quotient(x, n):
    return lax.shift_right_logical(x, jnp.int32(n.bit_length() - 1)) if n & (n - 1) == 0 else lax.div(x, jnp.int32(n))


def remainder(x, n):
    return x & (n - 1) if n & (n - 1) == 0 else lax.rem(x, jnp.int32(n))


def slots(owners, chips):
    flows = [o < chips - 1 for o in owners]

    def ahead(i, s):
        return flows[i] & ((owners[i] >= owners[s]) if i < s else (owners[i] > owners[s]))

    ranks = [
        sum(ahead(i, s).astype(jnp.int32) for i in range(SECTIONS) if i != s) for s in range(SECTIONS)
    ]
    firsts = []
    steps = jnp.int32(0)
    for s in range(SECTIONS):
        first = -LAG * owners[s]
        for j in range(SECTIONS):
            if j != s:
                pushed = (ranks[s] - ranks[j]) * PARTS - LAG * owners[j]
                first = jnp.where(ahead(j, s), jnp.maximum(first, pushed), first)
        firsts.append(first)
        steps = jnp.where(flows[s], jnp.maximum(steps, first + PARTS + LAG * (chips - 2)), steps)
    return firsts, steps


def owners_of(sections, col_tiles):
    return [quotient(sections[s], col_tiles * CORES) for s in range(SECTIONS)]


def lines(sections, col_tiles, chips):
    owners = owners_of(sections, col_tiles)
    return owners, [chips - 1 - o for o in owners]


def most_steps(chips):
    return SECTIONS * PARTS + LAG * (chips - 2)


def size_keys(rows, chips):
    most = most_steps(chips)
    if rows != 4 or chips > 4:
        return [(most, SECTIONS, SECTIONS)]
    return [
        (most - (SECTIONS - count) * PARTS, PAIR if count <= PAIR else SECTIONS, min(count + 1, SECTIONS))
        for count in range(1, SECTIONS + 1)
    ]


def table_rows(chips):
    own = 3 * most_steps(chips)
    words = own + 4 * SECTIONS
    return own, words, words + 1 + 2 * -(-most_steps(chips) // STEPS_A_WORD)


def largest(values):
    return functools.reduce(jnp.maximum, values)


def prepare_kernel(rows, col_tiles, row_tiles, chips, sections_in, pattern_in, values, *refs):
    masked = refs[:PARTS]
    table, which, sections, pattern, sems, small = refs[PARTS:]
    height = row_tiles * TILE // PARTS
    col = lax.axis_index("col")
    chip, core = quotient(col, CORES), remainder(col, CORES)
    most = most_steps(chips)

    def fetch(r):
        part, start = r * TILE // height, r * TILE % height
        block = values.at[r * TILE : (r + 1) * TILE, :]
        return pltpu.make_async_copy(block, masked[part].at[start : start + TILE, :], sems.at[r])

    lists = [
        pltpu.make_async_copy(sections_in, sections, small.at[0]),
        pltpu.make_async_copy(pattern_in, pattern, small.at[1]),
    ]
    for copy in lists:
        copy.start()
    for r in range(row_tiles):
        fetch(r).start()
    table[...] = jnp.full(table.shape, -1, jnp.int32)

    def note(row, item):
        table[pl.ds(row, 1), :] = jnp.full((1, table.shape[1]), item, jnp.int32)

    for copy in lists:
        copy.wait()
    up, down = lines(sections, col_tiles, chips)
    needed = jnp.int32(0)
    in_flow = [[jnp.int32(0)] * -(-most // STEPS_A_WORD) for _ in range(2)]
    for flow, line in enumerate((up, down)):
        place = chip if flow == 0 else chips - 1 - chip
        firsts, steps = slots(line, chips)
        needed = jnp.maximum(needed, steps)
        mine = core == flow
        for s in range(SECTIONS):

            @pl.when(mine & (line[s] == place) & (line[s] < chips - 1))
            def _():
                local = sections[s] - up[s] * (col_tiles * CORES)
                for part in range(PARTS):
                    note(firsts[s] + LAG * place + part, local)

            begin = firsts[s] + LAG * (place - 1)
            pair = (s + 1) * 17 << 4 * remainder(begin, STEPS_A_WORD)
            for word in range(len(in_flow[flow])):
                inside = (line[s] < place) & (quotient(begin, STEPS_A_WORD) == word)
                in_flow[flow][word] = in_flow[flow][word] + jnp.where(inside, pair, 0)

            @pl.when(line[s] < place)
            def _():
                for part in range(PARTS):
                    note(jnp.where(mine, most, 2 * most) + firsts[s] + LAG * (place - 1) + part, s)

    for s in range(SECTIONS):

        @pl.when(up[s] == chip)
        def _():
            note(3 * most + s, sections[s] - up[s] * (col_tiles * CORES))

    _, words, _ = table_rows(chips)
    tiles = jnp.int32(0)
    for s in range(SECTIONS):
        tiles = tiles + jnp.where(up[s] == chip, sections[s] - up[s] * (col_tiles * CORES) + 1 << 4 * s, 0)
    note(words, tiles)
    for word, (first, second) in enumerate(zip(*in_flow)):
        note(words + 1 + 2 * word, jnp.where(core == 0, first, second))
        note(words + 2 + 2 * word, jnp.where(core == 0, second, first))
    if rows == 4:
        note_rows(note, 3 * most + SECTIONS, sections, row_tiles, core)
    keys = size_keys(rows, chips)
    number = jnp.int32(0)
    if len(keys) > 1:
        owners = [quotient(sections[s], row_tiles) for s in range(SECTIONS)]
        counts = [sum((o == r).astype(jnp.int32) for o in owners) for r in range(4)]
        in_row = largest(counts)
        in_pair = largest([counts[i] + counts[j] for i, j in ((0, 1), (2, 3), (0, 2), (1, 3))])
        for key in keys[:-1]:
            fits = (needed <= key[0]) & (in_row <= key[1]) & (in_pair <= key[2])
            number = number + jnp.where(fits, 0, 1)
    which[0] = number

    for r in range(row_tiles):
        fetch(r).wait()
        part, start = r * TILE // height, r * TILE % height
        for c in range(col_tiles):

            @pl.when(pattern[c, r] == 0)
            def _():
                masked[part][start : start + TILE, c * TILE : (c + 1) * TILE] = jnp.zeros((TILE, TILE), BF16)


def rank_among(owners, s):
    return sum((owners[i] == owners[s]).astype(jnp.int32) for i in range(s)) + jnp.int32(0)


def bits(owner, first):
    x, y = remainder(owner, 2), quotient(owner, 2)
    return jnp.where(first, x, y), jnp.where(first, y, x)


def note_rows(note, start, sections, row_tiles, core):
    row = lax.axis_index("row")
    first = core == 0
    here = bits(row, first)
    owners = [quotient(sections[s], row_tiles) for s in range(SECTIONS)]
    pairs = [bits(o, first)[1] for o in owners]
    for s in range(SECTIONS):
        rank, slot = rank_among(owners, s), rank_among(pairs, s)

        @pl.when(owners[s] == row)
        def _():
            note(start + rank, sections[s] - owners[s] * row_tiles)

        @pl.when(pairs[s] == here[1])
        def _():
            note(start + SECTIONS + slot, rank + jnp.where(bits(owners[s], first)[0] == here[0], 0, SECTIONS))

        note(start + 2 * SECTIONS + s, slot + jnp.where(pairs[s] == here[1], 0, SECTIONS))


def own_rows_kernel(col_tiles, row_tiles, start, table, *refs):
    masked, outs = refs[:PARTS], refs[PARTS:]
    in_part = row_tiles // PARTS
    places = [(out, place) for out in outs for place in range(PAIR)]
    tiles = [jnp.max(table[start + i : start + i + 1, :]) for i in range(len(places))]
    for (out, place), tile in zip(places, tiles):
        local = jnp.maximum(tile, 0)
        for part in range(PARTS):
            first = pl.multiple_of((local - part * in_part) * TILE, TILE)

            @pl.when((tile >= 0) & (quotient(local, in_part) == part))
            def _():
                out[place] = masked[part][pl.ds(first, TILE), :]


def masked_rows_kernel(col_tiles, row_tiles, sections, *refs):
    masked, out = refs[:PARTS], refs[-1]
    row = lax.axis_index("row")
    in_part = row_tiles // PARTS
    for s in range(SECTIONS):
        owner = quotient(sections[s], row_tiles)
        local = sections[s] - owner * row_tiles
        out[s] = jnp.zeros(out.shape[1:], BF16)
        for part in range(PARTS):
            first = pl.multiple_of((local - part * in_part) * TILE, TILE)

            @pl.when((owner == row) & (quotient(local, in_part) == part))
            def _():
                out[s] = masked[part][pl.ds(first, TILE), :]


def near_rows_kernel(start, table, *refs):
    out = refs[-1]
    arrays = len(refs) // 2 - 1
    own, got = refs[:arrays], refs[arrays : 2 * arrays]
    sources = [jnp.max(table[start + i : start + i + 1, :]) for i in range(out.shape[0])]
    for i, source in enumerate(sources):
        rank = remainder(jnp.maximum(source, 0), SECTIONS)
        place = remainder(rank, PAIR)
        for number in range(arrays):
            wanted = (source >= 0) & (quotient(rank, PAIR) == number)

            @pl.when(wanted & (source < SECTIONS))
            def _():
                out[i] = own[number][place]

            @pl.when(wanted & (source >= SECTIONS))
            def _():
                out[i] = got[number][place]


def all_rows_kernel(start, table, near, far, out):
    sources = [jnp.max(table[start + s : start + s + 1, :]) for s in range(SECTIONS)]
    for s, source in enumerate(sources):
        slot = remainder(source, SECTIONS)

        @pl.when(source < SECTIONS)
        def _():
            out[s] = near[slot]

        @pl.when(source >= SECTIONS)
        def _():
            out[s] = far[slot]


def choose_kernel(col_tiles, t, table, masked, got, *refs):
    out = refs[-1]
    core = remainder(lax.axis_index("col"), CORES)
    tile = jnp.max(table[t : t + 1, :])
    local, owner = remainder(jnp.maximum(tile, 0), col_tiles), quotient(jnp.maximum(tile, 0), col_tiles)

    everything = slice(0, TILE)

    @pl.when((tile >= 0) & (owner == core))
    def _():
        copy_strips(masked, panel_columns(local), out, everything)

    @pl.when((tile >= 0) & (owner != core))
    def _():
        copy_strips(got, panel_columns(local), out, everything)

    if t >= LAG:

        @pl.when(tile < 0)
        def _():
            copy_strips(refs[0], everything, out, everything)


def panel_columns(s):
    return pl.ds(pl.multiple_of(s * TILE, TILE), TILE)


def arrivals(table, most, times, direct, passed):
    rows = [(entry * most + t, source) for t, d, p in zip(times, direct, passed) for entry, source in ((1, d), (2, p))]
    return [(jnp.max(table[row : row + 1, :]), source) for row, source in rows]


def copy_strips(source, taken, target, columns):
    @pl.loop(0, source.shape[0] // STRIP)
    def _(i):
        strip = pl.ds(pl.multiple_of(i * STRIP, STRIP), STRIP)
        target[strip, columns] = source[strip, taken]


def gather_kernel(col_tiles, chips, times, steps, table, *refs):
    refs, outs = refs[:-PARTS], refs[-PARTS:]
    core = remainder(lax.axis_index("col"), CORES)
    _, words, _ = table_rows(chips)
    tiles = jnp.max(table[words : words + 1, :])
    packed = [jnp.max(table[row : row + 1, :]) for row in range(words + 1, words + 1 + 2 * -(-steps // STEPS_A_WORD))]

    def entry(way, t):
        shift = jnp.int32(4 * (t % STEPS_A_WORD))
        return (lax.shift_right_logical(packed[2 * (t // STEPS_A_WORD) + way], shift) & 15) - 1

    for part in range(PARTS):
        masked, got = refs[2 * part : 2 * part + 2]
        count = len(times[part])
        ways = refs[2 * PARTS : 2 * PARTS + count], refs[2 * PARTS + count : 2 * PARTS + 2 * count]
        refs = refs[: 2 * PARTS] + refs[2 * PARTS + 2 * count :]
        left = outs[part]
        for s in range(SECTIONS):
            tile = (lax.shift_right_logical(tiles, jnp.int32(4 * s)) & 15) - 1
            local, owner = remainder(jnp.maximum(tile, 0), col_tiles), quotient(jnp.maximum(tile, 0), col_tiles)
            columns = slice(s * TILE, (s + 1) * TILE)

            @pl.when((tile >= 0) & (owner == core))
            def _():
                copy_strips(masked, panel_columns(local), left, columns)

            @pl.when((tile >= 0) & (owner != core))
            def _():
                copy_strips(got, panel_columns(local), left, columns)

        for way in range(2):
            for t, source in zip(times[part], ways[way]):
                s = entry(way, t)

                @pl.when(s >= 0)
                def _():
                    copy_strips(source, slice(0, TILE), left, panel_columns(jnp.maximum(s, 0)))

            s = entry(way, steps - PARTS + part)

            @pl.when(s >= 0)
            def _():
                left[:, panel_columns(jnp.maximum(s, 0))] = jnp.zeros((left.shape[0], TILE), BF16)


def early_product_kernel(*refs):
    panels, right, outs = refs[:PARTS], refs[PARTS], refs[PARTS + 1 :]
    for left, out in zip(panels, outs):
        for i in range(right.shape[1] // TILE):
            columns = slice(i * TILE, (i + 1) * TILE)
            out[:, columns] = jnp.dot(left[...], right[:, columns], preferred_element_type=jnp.float32)


def add_last_kernel(most, t, table, early, right, direct, passed, *refs):
    out, result, sems = refs[-3:]
    part, height = t % PARTS, early.shape[0]
    (here, _), (there, _) = arrivals(table, most, [t], [direct], [passed])
    some, both = jnp.maximum(here, there) >= 0, jnp.minimum(here, there) >= 0

    def write(pieces):
        copies = []
        for i in range(result.shape[0]):
            columns = slice(i * TILE, (i + 1) * TILE)
            for k in range(BLOCKS):
                rows = slice(k * (height // BLOCKS), (k + 1) * (height // BLOCKS))
                total = early[rows, columns]
                for s, piece in pieces:
                    total = total + jnp.dot(
                        piece[rows, :], right[panel_columns(s), columns], preferred_element_type=jnp.float32
                    )
                result[i, rows, :] = total.astype(BF16)
                target = out.at[part * height + rows.start : part * height + rows.stop, columns]
                copies.append(pltpu.make_async_copy(result.at[i, rows, :], target, sems.at[i, k]))
                copies[-1].start()
        for copy in copies:
            copy.wait()

    @pl.when(both)
    def _():
        write([(here, direct[...]), (there, passed[...])])

    @pl.when(some & jnp.logical_not(both))
    def _():
        write([(jnp.maximum(here, there), jnp.where(here >= 0, direct[...], passed[...]))])

    @pl.when(jnp.logical_not(some))
    def _():
        write([])


def mates(cols):
    return [(c, c ^ 1) for c in range(cols)]


def program(rows, cols, col_tiles, row_tiles, sizes, sections, table, *masked):
    steps, in_row, in_pair = sizes
    height, width = row_tiles * TILE, col_tiles * TILE
    chips = cols // CORES
    most = most_steps(chips)
    square = rows == 4
    tall = height // PARTS
    swap = mates(cols)
    ring = list(range(0, cols, CORES)) + list(range(cols - 1, 0, -CORES))
    around = [(ring[i], ring[(i + 1) % cols]) for i in range(cols)]
    rows_start = 3 * most + SECTIONS

    def stack(slots):
        return jax.ShapeDtypeStruct((slots, TILE, width), BF16)

    def turn(array, bits):
        pairs = [(r * cols + c, (r ^ bits[c % CORES]) * cols + c) for r in range(rows) for c in range(cols)]
        return lax.ppermute(array, ("row", "col"), pairs)

    got = [lax.ppermute(piece, "col", swap) for piece in masked]
    if square:
        own_rows = pl.pallas_call(
            functools.partial(own_rows_kernel, col_tiles, row_tiles, rows_start),
            out_shape=(stack(PAIR),) * (in_row // PAIR),
            in_specs=[VMEM] * (1 + PARTS),
            out_specs=(VMEM,) * (in_row // PAIR),
            compiler_params=PARAMS,
            name="own_rows",
        )(table, *masked)
        got_rows = [turn(own, (1, 2)) for own in own_rows]
    else:
        own_rows = pl.pallas_call(
            functools.partial(masked_rows_kernel, col_tiles, row_tiles),
            out_shape=stack(SECTIONS),
            in_specs=[SMEM] + [VMEM] * PARTS,
            out_specs=VMEM,
            compiler_params=PARAMS,
            name="masked_rows",
        )(sections, *masked)
        right = lax.psum(own_rows, "row")

    direct, passed = [], []
    for t in range(steps):
        operands = [table, masked[t % PARTS], got[t % PARTS]]
        specs = [VMEM] * len(operands)
        if t >= LAG:
            operands.append(direct[t - LAG])
            specs.append(VMEM)
        order = [sent] if t > 0 else []
        if t >= LAG + 2:
            order.append(passed[t - LAG - (1 if t == steps - 1 and in_row == PAIR else 2)])
        if square and t == in_row + 1:
            order += got_rows
        operands += order
        specs += [ANY] * len(order)
        sent = pl.pallas_call(
            functools.partial(choose_kernel, col_tiles, t),
            out_shape=jax.ShapeDtypeStruct((tall, TILE), BF16),
            in_specs=specs,
            out_specs=VMEM,
            compiler_params=PARAMS,
            name="choose",
        )(*operands)
        if t >= LAG:
            sent, piece = lax.optimization_barrier((sent, direct[t - LAG]))
            passed.append(lax.ppermute(piece, "col", swap))
        direct.append(lax.ppermute(sent, "col", around))
    passed.append(lax.ppermute(direct[-2], "col", swap))

    if square:
        near = pl.pallas_call(
            functools.partial(near_rows_kernel, rows_start + SECTIONS),
            out_shape=stack(in_pair),
            in_specs=[VMEM] + [VMEM] * (2 * len(own_rows)) + [ANY],
            out_specs=VMEM,
            compiler_params=PARAMS,
            name="near_rows",
        )(table, *own_rows, *got_rows, direct[1 if in_row == PAIR else 2])
        right = pl.pallas_call(
            functools.partial(all_rows_kernel, rows_start + 2 * SECTIONS),
            out_shape=stack(SECTIONS),
            in_specs=[VMEM] * 3,
            out_specs=VMEM,
            compiler_params=PARAMS,
            name="all_rows",
        )(table, *lax.optimization_barrier((near, turn(near, (2, 1)), sent))[:2])
    right = right.reshape(SECTIONS * TILE, width)

    panel = jax.ShapeDtypeStruct((tall, SECTIONS * TILE), BF16)
    partial = jax.ShapeDtypeStruct((tall, width), jnp.float32)
    result = jax.ShapeDtypeStruct((height, width), BF16)
    buffers = [pltpu.VMEM((col_tiles, tall, TILE), BF16), pltpu.SemaphoreType.DMA((col_tiles, BLOCKS))]
    times = [list(range(part, steps - PARTS, PARTS)) for part in range(PARTS)]
    piece, right = lax.optimization_barrier((sent, right))
    operands = [array for part in range(PARTS) for array in (masked[part], got[part])]
    for part in range(PARTS):
        operands += [direct[t] for t in times[part]] + [passed[t] for t in times[part]]
    operands.append(piece)
    left = pl.pallas_call(
        functools.partial(gather_kernel, col_tiles, chips, times, steps),
        out_shape=(panel,) * PARTS,
        in_specs=[VMEM] * len(operands) + [ANY],
        out_specs=(VMEM,) * PARTS,
        compiler_params=PARAMS,
        name="gather",
    )(table, *operands)
    *left, right, direct[-2] = lax.optimization_barrier((*left, right, direct[-2]))
    early = pl.pallas_call(
        early_product_kernel,
        out_shape=(partial,) * PARTS,
        in_specs=[VMEM] * (PARTS + 1),
        out_specs=(VMEM,) * PARTS,
        compiler_params=PARAMS,
        name="early_product",
    )(*left, right)
    direct[-1], passed[-1], *early = lax.optimization_barrier((direct[-1], passed[-1], *early))
    passed.append(lax.ppermute(direct[-1], "col", swap))

    def add_last(t, before):
        return pl.pallas_call(
            functools.partial(add_last_kernel, most, t),
            out_shape=result,
            in_specs=[VMEM] * 5 + [HBM] * len(before),
            out_specs=HBM,
            input_output_aliases={5: 0} if before else {},
            scratch_shapes=buffers,
            compiler_params=PARAMS,
            name="add_last",
        )(table, early[t % PARTS], right, direct[t], passed[t], *before)

    return add_last(steps - 1, (add_last(steps - 2, ()),))


def shards(rows, cols, values, pattern, sections):
    row_tiles, col_tiles = pattern.shape
    height, width = values.shape
    chips = cols // CORES
    most = most_steps(chips)
    panel = jax.ShapeDtypeStruct((height // PARTS, width), BF16)
    *masked, table, which = pl.pallas_call(
        functools.partial(prepare_kernel, rows, col_tiles, row_tiles, chips),
        out_shape=(panel,) * PARTS
        + (
            jax.ShapeDtypeStruct((-(-table_rows(chips)[2] // 8) * 8, 128), jnp.int32),
            jax.ShapeDtypeStruct((1,), jnp.int32),
        ),
        in_specs=[HBM, HBM, HBM],
        out_specs=(VMEM,) * (PARTS + 1) + (SMEM,),
        scratch_shapes=[
            pltpu.SMEM(sections.shape, jnp.int32),
            pltpu.SMEM((col_tiles, row_tiles), jnp.int32),
            pltpu.SemaphoreType.DMA((row_tiles,)),
            pltpu.SemaphoreType.DMA((2,)),
        ],
        compiler_params=pltpu.CompilerParams(vmem_limit_bytes=62 * 1024 * 1024),
        name="prepare",
    )(sections, pattern.T, values)
    branches = [
        functools.partial(program, rows, cols, col_tiles, row_tiles, sizes) for sizes in size_keys(rows, chips)
    ]
    return lax.switch(which[0], branches, sections, table, *masked)


def solution(mesh):
    body = functools.partial(shards, mesh.shape["row"], mesh.shape["col"])
    in_specs = (P("row", "col"), P("row", "col"), P())
    return jax.shard_map(body, mesh=mesh, in_specs=in_specs, out_specs=P("row", "col"), check_vma=False)
```

profile of v0, /device:TPU:0, one launch (start us, length us, event | category | flops | bytes accessed | tf_op | source)
XLA Modules:
  0.0 38.2 jit_solution(10613921554901319487)
XLA Ops:
  0.0 1.9 %prepare.1 = (bf16[512,512]{1,0:T(8,128)(2,1)S(1)}, bf16[512,512]{1,0:T(8,128)(2,1)S(1)}, s32[64,128]{1,0:T(8,128)S(1)}, s32[1]{0:T(128)}) custom-call(s32[4]{0:T(128)} %sections_in.1, s32[2,4]{1,0:T(2,128)} %bitcast.18, bf16[1024,512]{1,0:T(8,128)(2,1)} %values.1), custom_call_target="tpu_custom_call" | custom-call | tf_op jit(solution)/shard_map/prepare/pallas_call | solution.py:549
  2.6 35.4 %conditional.1 = (bf16[1024,512]{1,0:T(8,128)(2,1)}) conditional(s32[]{:T(128)} %bitcast.5, (bf16[512,512]{1,0:T(8,128)(2,1)S(1)}, bf16[512,512]{1,0:T(8,128)(2,1)S(1)}, s32[64,128]{1,0:T(8,128)S(1)}) %tuple.61, (bf16[512,512]{1,0:T(8,128)(2,1)S(1)}, bf16[512,512]{1,0:T(8,128)(2,1)S(1)}, ...), branch_computations={%region_0.0_spmd, %region_1.0_spmd, %region_2.0_spmd, %region_3.0_... | conditional | bytes 37749904 | solution.py:570
  2.6 0.5 %collective-permute-start.17 = (bf16[512,512]{1,0:T(8,128)(2,1)S(1)}, bf16[512,512]{1,0:T(8,128)(2,1)S(1)}, u32[]{:S(2)}, u32[]{:S(2)}) collective-permute-start(bf16[512,512]{1,0:T(8,128)(2,1)S(1)} %get-tuple-element.63.masked.refs_0_), channel_id=1, source_target_pairs={{0,1},{1,0},{2,3},{3,2},{4,5},{5,4},{6,7},{7,6},{8,9},{9,8},{10,11... | collective-permute-start | bytes 1572872 | tf_op jit(solution)/shard_map/cond/branch_1_fun/ppermute | solution.py:429
  3.2 0.2 own_rows.5.refs_0_
  3.4 3.0 %collective-permute-start.20 = (bf16[2,256,512]{2,1,0:T(8,128)(2,1)S(1)}, bf16[2,256,512]{2,1,0:T(8,128)(2,1)S(1)}, u32[]{:S(2)}, u32[]{:S(2)}) collective-permute-start(bf16[2,256,512]{2,1,0:T(8,128)(2,1)S(1)} %own_rows.5.refs_0_), channel_id=1, source_target_pairs={{0,8},{1,17},{2,10},{3,19},{4,12},{5,21},{6,14},{7,23},{8,0},{9,25... | collective-permute-start | bytes 1572872 | tf_op jit(solution)/shard_map/cond/branch_1_fun/ppermute | solution.py:427
  6.4 0.2 choose.42.refs_0_
  6.7 1.6 %collective-permute-start.19 = (bf16[512,256]{1,0:T(8,128)(2,1)S(1)}, bf16[512,256]{1,0:T(8,128)(2,1)S(1)}, u32[]{:S(2)}, u32[]{:S(2)}) collective-permute-start(bf16[512,256]{1,0:T(8,128)(2,1)S(1)} %choose.42.refs_0_), channel_id=1, source_target_pairs={{0,2},{2,4},{4,6},{6,7},{7,5},{5,3},{3,1},{1,0},{8,10},{10,12},{12... | collective-permute-start | bytes 786440 | tf_op jit(solution)/shard_map/cond/branch_1_fun/ppermute | solution.py:476
  8.3 0.2 choose.43.refs_1_
  8.5 1.6 %collective-permute-start.18 = (bf16[512,256]{1,0:T(8,128)(2,1)S(1)}, bf16[512,256]{1,0:T(8,128)(2,1)S(1)}, u32[]{:S(2)}, u32[]{:S(2)}) collective-permute-start(bf16[512,256]{1,0:T(8,128)(2,1)S(1)} %choose.43.refs_1_), channel_id=1, source_target_pairs={{0,2},{2,4},{4,6},{6,7},{7,5},{5,3},{3,1},{1,0},{8,10},{10,12},{12... | collective-permute-start | bytes 786440 | tf_op jit(solution)/shard_map/cond/branch_1_fun/ppermute | solution.py:476
  10.1 2.1 %collective-permute-done.19.refs_0_.refs_4_ = bf16[512,256]{1,0:T(8,128)(2,1)S(1)} collective-permute-done((bf16[512,256]{1,0:T(8,128)(2,1)S(1)}, bf16[512,256]{1,0:T(8,128)(2,1)S(1)}, u32[]{:S(2)}, u32[]{:S(2)}) %collective-permute-start.19) | collective-permute-done | bytes 262176 | tf_op jit(solution)/shard_map/cond/branch_1_fun/ppermute | solution.py:476
  12.2 0.2 choose.44.refs_1_
  12.4 2.5 %collective-permute-start.22 = (bf16[512,256]{1,0:T(8,128)(2,1)S(1)}, bf16[512,256]{1,0:T(8,128)(2,1)S(1)}, u32[]{:S(2)}, u32[]{:S(2)}) collective-permute-start(bf16[512,256]{1,0:T(8,128)(2,1)S(1)} %choose.44.refs_1_), channel_id=1, source_target_pairs={{0,2},{2,4},{4,6},{6,7},{7,5},{5,3},{3,1},{1,0},{8,10},{10,12},{12... | collective-permute-start | bytes 786440 | tf_op jit(solution)/shard_map/cond/branch_1_fun/ppermute | solution.py:476
  15.2 2.5 %collective-permute-start.21 = (bf16[512,256]{1,0:T(8,128)(2,1)S(1)}, bf16[512,256]{1,0:T(8,128)(2,1)S(1)}, u32[]{:S(2)}, u32[]{:S(2)}) collective-permute-start(bf16[512,256]{1,0:T(8,128)(2,1)S(1)} %choose.45.refs_1_), channel_id=1, source_target_pairs={{0,2},{2,4},{4,6},{6,7},{7,5},{5,3},{3,1},{1,0},{8,10},{10,12},{12... | collective-permute-start | bytes 786440 | tf_op jit(solution)/shard_map/cond/branch_1_fun/ppermute | solution.py:476
  17.7 0.3 near_rows.5.near
  18.0 1.6 %collective-permute-start.34 = (bf16[3,256,512]{2,1,0:T(8,128)(2,1)S(1)}, bf16[3,256,512]{2,1,0:T(8,128)(2,1)S(1)}, u32[]{:S(2)}, u32[]{:S(2)}) collective-permute-start(bf16[3,256,512]{2,1,0:T(8,128)(2,1)S(1)} %near_rows.5.near), channel_id=1, source_target_pairs={{0,16},{1,9},{2,18},{3,11},{4,20},{5,13},{6,22},{7,15},{8,24},{9,1... | collective-permute-start | bytes 2359304 | tf_op jit(solution)/shard_map/cond/branch_1_fun/ppermute | solution.py:427
  19.6 0.2 choose.46.refs_1_
  19.8 1.7 %collective-permute-start.26 = (bf16[512,256]{1,0:T(8,128)(2,1)S(1)}, bf16[512,256]{1,0:T(8,128)(2,1)S(1)}, u32[]{:S(2)}, u32[]{:S(2)}) collective-permute-start(bf16[512,256]{1,0:T(8,128)(2,1)S(1)} %choose.46.refs_1_), channel_id=1, source_target_pairs={{0,2},{2,4},{4,6},{6,7},{7,5},{5,3},{3,1},{1,0},{8,10},{10,12},{12... | collective-permute-start | bytes 786440 | tf_op jit(solution)/shard_map/cond/branch_1_fun/ppermute | solution.py:476
  21.6 0.2 choose.47.refs_1_
  21.8 2.5 %collective-permute-start.25 = (bf16[512,256]{1,0:T(8,128)(2,1)S(1)}, bf16[512,256]{1,0:T(8,128)(2,1)S(1)}, u32[]{:S(2)}, u32[]{:S(2)}) collective-permute-start(bf16[512,256]{1,0:T(8,128)(2,1)S(1)} %choose.47.refs_1_), channel_id=1, source_target_pairs={{0,2},{2,4},{4,6},{6,7},{7,5},{5,3},{3,1},{1,0},{8,10},{10,12},{12... | collective-permute-start | bytes 786440 | tf_op jit(solution)/shard_map/cond/branch_1_fun/ppermute | solution.py:476
  24.3 1.1 %collective-permute-done.26.refs_0_.refs_6_ = bf16[512,256]{1,0:T(8,128)(2,1)S(1)} collective-permute-done((bf16[512,256]{1,0:T(8,128)(2,1)S(1)}, bf16[512,256]{1,0:T(8,128)(2,1)S(1)}, u32[]{:S(2)}, u32[]{:S(2)}) %collective-permute-start.26) | collective-permute-done | bytes 262176 | tf_op jit(solution)/shard_map/cond/branch_1_fun/ppermute | solution.py:476
  25.4 0.2 choose.48.refs_1_
  25.7 2.5 %collective-permute-start.30 = (bf16[512,256]{1,0:T(8,128)(2,1)S(1)}, bf16[512,256]{1,0:T(8,128)(2,1)S(1)}, u32[]{:S(2)}, u32[]{:S(2)}) collective-permute-start(bf16[512,256]{1,0:T(8,128)(2,1)S(1)} %choose.48.refs_1_), channel_id=1, source_target_pairs={{0,2},{2,4},{4,6},{6,7},{7,5},{5,3},{3,1},{1,0},{8,10},{10,12},{12... | collective-permute-start | bytes 786440 | tf_op jit(solution)/shard_map/cond/branch_1_fun/ppermute | solution.py:476
  28.3 0.2 choose.49.refs_16_
  28.5 0.6 %collective-permute-start.33 = (bf16[512,256]{1,0:T(8,128)(2,1)S(1)}, bf16[512,256]{1,0:T(8,128)(2,1)S(1)}, u32[]{:S(2)}, u32[]{:S(2)}) collective-permute-start(bf16[512,256]{1,0:T(8,128)(2,1)S(1)} %collective-permute-done.25.refs_0_.refs_12_), channel_id=1, source_target_pairs={{0,1},{1,0},{2,3},{3,2},{4,5},{5,4},{6,7},{7,6},{8,9},{9,8},{10,11... | collective-permute-start | bytes 786440 | tf_op jit(solution)/shard_map/cond/branch_1_fun/ppermute | solution.py:475
  29.1 2.0 %collective-permute-start.29 = (bf16[512,256]{1,0:T(8,128)(2,1)S(1)}, bf16[512,256]{1,0:T(8,128)(2,1)S(1)}, u32[]{:S(2)}, u32[]{:S(2)}) collective-permute-start(bf16[512,256]{1,0:T(8,128)(2,1)S(1)} %choose.49.refs_16_), channel_id=1, source_target_pairs={{0,2},{2,4},{4,6},{6,7},{7,5},{5,3},{3,1},{1,0},{8,10},{10,12},{12... | collective-permute-start | bytes 786440 | tf_op jit(solution)/shard_map/cond/branch_1_fun/ppermute | solution.py:476
  31.1 1.1 %collective-permute-done.30.direct = bf16[512,256]{1,0:T(8,128)(2,1)S(1)} collective-permute-done((bf16[512,256]{1,0:T(8,128)(2,1)S(1)}, bf16[512,256]{1,0:T(8,128)(2,1)S(1)}, u32[]{:S(2)}, u32[]{:S(2)}) %collective-permute-start.30) | collective-permute-done | bytes 262176 | tf_op jit(solution)/shard_map/cond/branch_1_fun/ppermute | solution.py:476
  32.2 0.3 all_rows.5
  32.5 0.6 %gather.5 = (bf16[512,1024]{1,0:T(8,128)(2,1)S(1)}, bf16[512,1024]{1,0:T(8,128)(2,1)S(1)}) custom-call(s32[64,128]{1,0:T(8,128)S(1)} %get-tuple-element.61.table, bf16[512,512]{1,0:T(8,128)(2,1)S(1)} %get-tuple-element.63.masked.refs_0_, bf16[512,512]{1,0:T(8,128)(2,1)S(1)} %collective-permute-done.17.got.refs_1_, ...), custom_call_target="tpu_custom_call" | custom-call | tf_op jit(solution)/shard_map/cond/branch_1_fun/gather/pallas_call | solution.py:508
  33.2 1.2 %early_product.5 = (f32[512,512]{1,0:T(8,128)S(1)}, f32[512,512]{1,0:T(8,128)S(1)}) custom-call(bf16[512,1024]{1,0:T(8,128)(2,1)S(1)} %get-tuple-element.82.refs_0_, bf16[512,1024]{1,0:T(8,128)(2,1)S(1)} %get-tuple-element.83.refs_1_, bf16[1024,512]{1,0:T(8,128)(2,1)S(1)} %bitcast.15), custom_call_target="tpu_custom_call" | custom-call | tf_op jit(solution)/shard_map/cond/branch_1_fun/early_product/pallas_call | solution.py:517
  34.4 0.5 %collective-permute-done.29.direct = bf16[512,256]{1,0:T(8,128)(2,1)S(1)} collective-permute-done((bf16[512,256]{1,0:T(8,128)(2,1)S(1)}, bf16[512,256]{1,0:T(8,128)(2,1)S(1)}, u32[]{:S(2)}, u32[]{:S(2)}) %collective-permute-start.29) | collective-permute-done | bytes 262176 | tf_op jit(solution)/shard_map/cond/branch_1_fun/ppermute | solution.py:476
  35.0 1.3 %add_last.10.refs_0_ = bf16[1024,512]{1,0:T(8,128)(2,1)} custom-call(s32[64,128]{1,0:T(8,128)S(1)} %get-tuple-element.61.table, f32[512,512]{1,0:T(8,128)S(1)} %get-tuple-element.89.early, bf16[1024,512]{1,0:T(8,128)(2,1)S(1)} %bitcast.16, bf16[512,256]{1,0:T(8,128)(2,1)S(1)} %collective-permute-done.30.direct, ...), custom_call_target="tpu_custom_call" | custom-call | tf_op jit(solution)/shard_map/cond/branch_1_fun/add_last/pallas_call | solution.py:529
  36.5 1.3 %add_last.11 = bf16[1024,512]{1,0:T(8,128)(2,1)} custom-call(s32[64,128]{1,0:T(8,128)S(1)} %get-tuple-element.61.table, f32[512,512]{1,0:T(8,128)S(1)} %get-tuple-element.87.early, bf16[1024,512]{1,0:T(8,128)(2,1)S(1)} %bitcast.17, bf16[512,256]{1,0:T(8,128)(2,1)S(1)} %collective-permute-done.29.direct, ...), custom_call_target="tpu_custom_call", output_to_operand_aliasing={{}: (5, {})} | custom-call | tf_op jit(solution)/shard_map/cond/branch_1_fun/add_last/pallas_call | solution.py:529
  (25 shorter events, 0.9 us)
Async XLA Ops:
  2.6 3.8 %collective-permute-start.17 = (bf16[512,512]{1,0:T(8,128)(2,1)S(1)}, bf16[512,512]{1,0:T(8,128)(2,1)S(1)}, u32[]{:S(2)}, u32[]{:S(2)}) collective-permute-start(bf16[512,512]{1,0:T(8,128)(2,1)S(1)} %get-tuple-element.63.masked.refs_0_), channel_id=1, source_target_pairs={{0,1},{1,0},{2,3},{3,2},{4,5},{5,4},{6,7},{7,6},{8,9},{9,8},{10,11... | collective-permute-start | bytes 1572872 | tf_op jit(solution)/shard_map/cond/branch_1_fun/ppermute | solution.py:429
  3.1 5.1 %collective-permute-start.16 = (bf16[512,512]{1,0:T(8,128)(2,1)S(1)}, bf16[512,512]{1,0:T(8,128)(2,1)S(1)}, u32[]{:S(2)}, u32[]{:S(2)}) collective-permute-start(bf16[512,512]{1,0:T(8,128)(2,1)S(1)} %get-tuple-element.62.masked.refs_1_.refs_2_), channel_id=1, source_target_pairs={{0,1},{1,0},{2,3},{3,2},{4,5},{5,4},{6,7},{7,6},{8,9},{9,8},{10,11... | collective-permute-start | bytes 1572872 | tf_op jit(solution)/shard_map/cond/branch_1_fun/ppermute | solution.py:429
  3.4 11.5 %collective-permute-start.20 = (bf16[2,256,512]{2,1,0:T(8,128)(2,1)S(1)}, bf16[2,256,512]{2,1,0:T(8,128)(2,1)S(1)}, u32[]{:S(2)}, u32[]{:S(2)}) collective-permute-start(bf16[2,256,512]{2,1,0:T(8,128)(2,1)S(1)} %own_rows.5.refs_0_), channel_id=1, source_target_pairs={{0,8},{1,17},{2,10},{3,19},{4,12},{5,21},{6,14},{7,23},{8,0},{9,25... | collective-permute-start | bytes 1572872 | tf_op jit(solution)/shard_map/cond/branch_1_fun/ppermute | solution.py:427
  6.7 5.5 %collective-permute-start.19 = (bf16[512,256]{1,0:T(8,128)(2,1)S(1)}, bf16[512,256]{1,0:T(8,128)(2,1)S(1)}, u32[]{:S(2)}, u32[]{:S(2)}) collective-permute-start(bf16[512,256]{1,0:T(8,128)(2,1)S(1)} %choose.42.refs_0_), channel_id=1, source_target_pairs={{0,2},{2,4},{4,6},{6,7},{7,5},{5,3},{3,1},{1,0},{8,10},{10,12},{12... | collective-permute-start | bytes 786440 | tf_op jit(solution)/shard_map/cond/branch_1_fun/ppermute | solution.py:476
  8.5 6.4 %collective-permute-start.18 = (bf16[512,256]{1,0:T(8,128)(2,1)S(1)}, bf16[512,256]{1,0:T(8,128)(2,1)S(1)}, u32[]{:S(2)}, u32[]{:S(2)}) collective-permute-start(bf16[512,256]{1,0:T(8,128)(2,1)S(1)} %choose.43.refs_1_), channel_id=1, source_target_pairs={{0,2},{2,4},{4,6},{6,7},{7,5},{5,3},{3,1},{1,0},{8,10},{10,12},{12... | collective-permute-start | bytes 786440 | tf_op jit(solution)/shard_map/cond/branch_1_fun/ppermute | solution.py:476
  12.4 7.2 %collective-permute-start.22 = (bf16[512,256]{1,0:T(8,128)(2,1)S(1)}, bf16[512,256]{1,0:T(8,128)(2,1)S(1)}, u32[]{:S(2)}, u32[]{:S(2)}) collective-permute-start(bf16[512,256]{1,0:T(8,128)(2,1)S(1)} %choose.44.refs_1_), channel_id=1, source_target_pairs={{0,2},{2,4},{4,6},{6,7},{7,5},{5,3},{3,1},{1,0},{8,10},{10,12},{12... | collective-permute-start | bytes 786440 | tf_op jit(solution)/shard_map/cond/branch_1_fun/ppermute | solution.py:476
  14.9 4.7 %collective-permute-start.23 = (bf16[512,256]{1,0:T(8,128)(2,1)S(1)}, bf16[512,256]{1,0:T(8,128)(2,1)S(1)}, u32[]{:S(2)}, u32[]{:S(2)}) collective-permute-start(bf16[512,256]{1,0:T(8,128)(2,1)S(1)} %collective-permute-done.19.refs_0_.refs_4_), channel_id=1, source_target_pairs={{0,1},{1,0},{2,3},{3,2},{4,5},{5,4},{6,7},{7,6},{8,9},{9,8},{10,11... | collective-permute-start | bytes 786440 | tf_op jit(solution)/shard_map/cond/branch_1_fun/ppermute | solution.py:475
  15.2 6.4 %collective-permute-start.21 = (bf16[512,256]{1,0:T(8,128)(2,1)S(1)}, bf16[512,256]{1,0:T(8,128)(2,1)S(1)}, u32[]{:S(2)}, u32[]{:S(2)}) collective-permute-start(bf16[512,256]{1,0:T(8,128)(2,1)S(1)} %choose.45.refs_1_), channel_id=1, source_target_pairs={{0,2},{2,4},{4,6},{6,7},{7,5},{5,3},{3,1},{1,0},{8,10},{10,12},{12... | collective-permute-start | bytes 786440 | tf_op jit(solution)/shard_map/cond/branch_1_fun/ppermute | solution.py:476
  17.7 3.9 %collective-permute-start.24 = (bf16[512,256]{1,0:T(8,128)(2,1)S(1)}, bf16[512,256]{1,0:T(8,128)(2,1)S(1)}, u32[]{:S(2)}, u32[]{:S(2)}) collective-permute-start(bf16[512,256]{1,0:T(8,128)(2,1)S(1)} %collective-permute-done.18.refs_0_.refs_2_.refs_10_), channel_id=1, source_target_pairs={{0,1},{1,0},{2,3},{3,2},{4,5},{5,4},{6,7},{7,6},{8,9},{9,8},{10,11... | collective-permute-start | bytes 786440 | tf_op jit(solution)/shard_map/cond/branch_1_fun/ppermute | solution.py:475
  18.0 14.2 %collective-permute-start.34 = (bf16[3,256,512]{2,1,0:T(8,128)(2,1)S(1)}, bf16[3,256,512]{2,1,0:T(8,128)(2,1)S(1)}, u32[]{:S(2)}, u32[]{:S(2)}) collective-permute-start(bf16[3,256,512]{2,1,0:T(8,128)(2,1)S(1)} %near_rows.5.near), channel_id=1, source_target_pairs={{0,16},{1,9},{2,18},{3,11},{4,20},{5,13},{6,22},{7,15},{8,24},{9,1... | collective-permute-start | bytes 2359304 | tf_op jit(solution)/shard_map/cond/branch_1_fun/ppermute | solution.py:427
  19.8 5.6 %collective-permute-start.26 = (bf16[512,256]{1,0:T(8,128)(2,1)S(1)}, bf16[512,256]{1,0:T(8,128)(2,1)S(1)}, u32[]{:S(2)}, u32[]{:S(2)}) collective-permute-start(bf16[512,256]{1,0:T(8,128)(2,1)S(1)} %choose.46.refs_1_), channel_id=1, source_target_pairs={{0,2},{2,4},{4,6},{6,7},{7,5},{5,3},{3,1},{1,0},{8,10},{10,12},{12... | collective-permute-start | bytes 786440 | tf_op jit(solution)/shard_map/cond/branch_1_fun/ppermute | solution.py:476
  21.5 3.9 %collective-permute-start.27 = (bf16[512,256]{1,0:T(8,128)(2,1)S(1)}, bf16[512,256]{1,0:T(8,128)(2,1)S(1)}, u32[]{:S(2)}, u32[]{:S(2)}) collective-permute-start(bf16[512,256]{1,0:T(8,128)(2,1)S(1)} %collective-permute-done.22.refs_0_.refs_5_), channel_id=1, source_target_pairs={{0,1},{1,0},{2,3},{3,2},{4,5},{5,4},{6,7},{7,6},{8,9},{9,8},{10,11... | collective-permute-start | bytes 786440 | tf_op jit(solution)/shard_map/cond/branch_1_fun/ppermute | solution.py:475
  21.8 6.4 %collective-permute-start.25 = (bf16[512,256]{1,0:T(8,128)(2,1)S(1)}, bf16[512,256]{1,0:T(8,128)(2,1)S(1)}, u32[]{:S(2)}, u32[]{:S(2)}) collective-permute-start(bf16[512,256]{1,0:T(8,128)(2,1)S(1)} %choose.47.refs_1_), channel_id=1, source_target_pairs={{0,2},{2,4},{4,6},{6,7},{7,5},{5,3},{3,1},{1,0},{8,10},{10,12},{12... | collective-permute-start | bytes 786440 | tf_op jit(solution)/shard_map/cond/branch_1_fun/ppermute | solution.py:476
  25.7 2.6 %collective-permute-start.28 = (bf16[512,256]{1,0:T(8,128)(2,1)S(1)}, bf16[512,256]{1,0:T(8,128)(2,1)S(1)}, u32[]{:S(2)}, u32[]{:S(2)}) collective-permute-start(bf16[512,256]{1,0:T(8,128)(2,1)S(1)} %collective-permute-done.26.refs_0_.refs_6_), channel_id=1, source_target_pairs={{0,1},{1,0},{2,3},{3,2},{4,5},{5,4},{6,7},{7,6},{8,9},{9,8},{10,11... | collective-permute-start | bytes 786440 | tf_op jit(solution)/shard_map/cond/branch_1_fun/ppermute | solution.py:475
  25.7 6.4 %collective-permute-start.30 = (bf16[512,256]{1,0:T(8,128)(2,1)S(1)}, bf16[512,256]{1,0:T(8,128)(2,1)S(1)}, u32[]{:S(2)}, u32[]{:S(2)}) collective-permute-start(bf16[512,256]{1,0:T(8,128)(2,1)S(1)} %choose.48.refs_1_), channel_id=1, source_target_pairs={{0,2},{2,4},{4,6},{6,7},{7,5},{5,3},{3,1},{1,0},{8,10},{10,12},{12... | collective-permute-start | bytes 786440 | tf_op jit(solution)/shard_map/cond/branch_1_fun/ppermute | solution.py:476
  28.2 4.3 %collective-permute-start.32 = (bf16[512,256]{1,0:T(8,128)(2,1)S(1)}, bf16[512,256]{1,0:T(8,128)(2,1)S(1)}, u32[]{:S(2)}, u32[]{:S(2)}) collective-permute-start(bf16[512,256]{1,0:T(8,128)(2,1)S(1)} %collective-permute-done.21.refs_0_.refs_11_), channel_id=1, source_target_pairs={{0,1},{1,0},{2,3},{3,2},{4,5},{5,4},{6,7},{7,6},{8,9},{9,8},{10,11... | collective-permute-start | bytes 786440 | tf_op jit(solution)/shard_map/cond/branch_1_fun/ppermute | solution.py:475
  28.5 4.0 %collective-permute-start.33 = (bf16[512,256]{1,0:T(8,128)(2,1)S(1)}, bf16[512,256]{1,0:T(8,128)(2,1)S(1)}, u32[]{:S(2)}, u32[]{:S(2)}) collective-permute-start(bf16[512,256]{1,0:T(8,128)(2,1)S(1)} %collective-permute-done.25.refs_0_.refs_12_), channel_id=1, source_target_pairs={{0,1},{1,0},{2,3},{3,2},{4,5},{5,4},{6,7},{7,6},{8,9},{9,8},{10,11... | collective-permute-start | bytes 786440 | tf_op jit(solution)/shard_map/cond/branch_1_fun/ppermute | solution.py:475
  29.1 5.9 %collective-permute-start.29 = (bf16[512,256]{1,0:T(8,128)(2,1)S(1)}, bf16[512,256]{1,0:T(8,128)(2,1)S(1)}, u32[]{:S(2)}, u32[]{:S(2)}) collective-permute-start(bf16[512,256]{1,0:T(8,128)(2,1)S(1)} %choose.49.refs_16_), channel_id=1, source_target_pairs={{0,2},{2,4},{4,6},{6,7},{7,5},{5,3},{3,1},{1,0},{8,10},{10,12},{12... | collective-permute-start | bytes 786440 | tf_op jit(solution)/shard_map/cond/branch_1_fun/ppermute | solution.py:476
  32.1 2.8 %collective-permute-start.31 = (bf16[512,256]{1,0:T(8,128)(2,1)S(1)}, bf16[512,256]{1,0:T(8,128)(2,1)S(1)}, u32[]{:S(2)}, u32[]{:S(2)}) collective-permute-start(bf16[512,256]{1,0:T(8,128)(2,1)S(1)} %collective-permute-done.30.direct), channel_id=1, source_target_pairs={{0,1},{1,0},{2,3},{3,2},{4,5},{5,4},{6,7},{7,6},{8,9},{9,8},{10,11... | collective-permute-start | bytes 786440 | tf_op jit(solution)/shard_map/cond/branch_1_fun/ppermute | solution.py:477
  35.0 1.5 %collective-permute-start.35 = (bf16[512,256]{1,0:T(8,128)(2,1)S(1)}, bf16[512,256]{1,0:T(8,128)(2,1)S(1)}, u32[]{:S(2)}, u32[]{:S(2)}) collective-permute-start(bf16[512,256]{1,0:T(8,128)(2,1)S(1)} %collective-permute-done.29.direct), channel_id=1, source_target_pairs={{0,1},{1,0},{2,3},{3,2},{4,5},{5,4},{6,7},{7,6},{8,9},{9,8},{10,11... | collective-permute-start | bytes 786440 | tf_op jit(solution)/shard_map/cond/branch_1_fun/ppermute | solution.py:526
where the time goes:
time: 38.3 us; the launch traced here: 38.2 us
  starting transfers between devices  22.8 us (60%)
  Pallas kernels  9.03 us (24%)
  waiting for transfers between devices  5.09 us (13%)
  between operations  0.84 us (2%)
  loops' own time  0.41 us (1%)
    ppermute x8, starting transfers between devices, program(): direct.append(lax.ppermute(sent, 'col', around))  16.8 us
    ppermute x8, waiting for transfers between devices, program(): direct.append(lax.ppermute(sent, 'col', around))  4.87 us
    ppermute x2, starting transfers between devices, turn(): return lax.ppermute(array, ('row', 'col'), pairs)  4.57 us
    pallas_call x2, Pallas kernels, add_last(): pl.pallas_call(functools.partial(add_last_kernel, most, t), out_shape=res...  2.53 us
    pallas_call x1, Pallas kernels, shards(): pl.pallas_call(functools.partial(prepare_kernel, rows, col_tiles, row_til...  1.91 us
    pallas_call x8, Pallas kernels, program(): pl.pallas_call(functools.partial(choose_kernel, col_tiles, t), out_shape=...  1.89 us
    pallas_call x1, Pallas kernels, program(): pl.pallas_call(early_product_kernel, out_shape=(partial,) * PARTS, in_spe...  1.25 us
  transfers between devices with their start and end apart: 20, of which 7 were waited for; matrix products, arithmetic and copies ran while one was open for 0% of the time, Pallas kernels for 15%

commit v1 on v0

--- a/solution.py
+++ b/solution.py
@@ -213,7 +213,7 @@
     masked, outs = refs[:PARTS], refs[PARTS:]
     in_part = row_tiles // PARTS
     places = [(out, place) for out in outs for place in range(PAIR)]
-    tiles = [jnp.max(table[start + i : start + i + 1, :]) for i in range(len(places))]
+    tiles = [jnp.max(table[start + i : start + i + 1, :1]) for i in range(len(places))]
     for (out, place), tile in zip(places, tiles):
         local = jnp.maximum(tile, 0)
         for part in range(PARTS):
@@ -244,7 +244,7 @@
     out = refs[-1]
     arrays = len(refs) // 2 - 1
     own, got = refs[:arrays], refs[arrays : 2 * arrays]
-    sources = [jnp.max(table[start + i : start + i + 1, :]) for i in range(out.shape[0])]
+    sources = [jnp.max(table[start + i : start + i + 1, :1]) for i in range(out.shape[0])]
     for i, source in enumerate(sources):
         rank = remainder(jnp.maximum(source, 0), SECTIONS)
         place = remainder(rank, PAIR)
@@ -261,7 +261,7 @@
 
 
 def all_rows_kernel(start, table, near, far, out):
-    sources = [jnp.max(table[start + s : start + s + 1, :]) for s in range(SECTIONS)]
+    sources = [jnp.max(table[start + s : start + s + 1, :1]) for s in range(SECTIONS)]
     for s, source in enumerate(sources):
         slot = remainder(source, SECTIONS)
 
@@ -277,7 +277,7 @@
 def choose_kernel(col_tiles, t, table, masked, got, *refs):
     out = refs[-1]
     core = remainder(lax.axis_index("col"), CORES)
-    tile = jnp.max(table[t : t + 1, :])
+    tile = jnp.max(table[t : t + 1, :1])
     local, owner = remainder(jnp.maximum(tile, 0), col_tiles), quotient(jnp.maximum(tile, 0), col_tiles)
 
     everything = slice(0, TILE)
@@ -303,7 +303,7 @@
 
 def arrivals(table, most, times, direct, passed):
     rows = [(entry * most + t, source) for t, d, p in zip(times, direct, passed) for entry, source in ((1, d), (2, p))]
-    return [(jnp.max(table[row : row + 1, :]), source) for row, source in rows]
+    return [(jnp.max(table[row : row + 1, :1]), source) for row, source in rows]
 
 
 def copy_strips(source, taken, target, columns):
@@ -317,8 +317,8 @@
     refs, outs = refs[:-PARTS], refs[-PARTS:]
     core = remainder(lax.axis_index("col"), CORES)
     _, words, _ = table_rows(chips)
-    tiles = jnp.max(table[words : words + 1, :])
-    packed = [jnp.max(table[row : row + 1, :]) for row in range(words + 1, words + 1 + 2 * -(-steps // STEPS_A_WORD))]
+    tiles = jnp.max(table[words : words + 1, :1])
+    packed = [jnp.max(table[row : row + 1, :1]) for row in range(words + 1, words + 1 + 2 * -(-steps // STEPS_A_WORD))]
 
     def entry(way, t):
         shift = jnp.int32(4 * (t % STEPS_A_WORD))

time: 38.3 us -> 37.2 us (0.971)
  Pallas kernels: 9.03 us -> 6.37 us
  waiting for transfers between devices: 5.09 us -> 6.36 us
    pallas_call x8, Pallas kernels: 1.89 us -> 0.61 us  [program(): pl.pallas_call(functools.partial(choose_kernel, col_tiles, t), out_shape=...]
    ppermute x8, waiting for transfers between devices: 4.87 us -> 5.76 us  [program(): direct.append(lax.ppermute(sent, 'col', around))]
    pallas_call x2, Pallas kernels: 2.53 us -> 1.77 us  [add_last(): pl.pallas_call(functools.partial(add_last_kernel, most, t), out_shape=res...]
  transfers between devices with their start and end apart: 20 -> 20, of which waited for: 7 -> 8; matrix products, arithmetic and copies ran while one was open for 0% -> 0% of each run, Pallas kernels for 15% -> 10%
where the time goes in v1:
time: 37.2 us; the launch traced here: 36.9 us
  starting transfers between devices  22.9 us (62%)
  Pallas kernels  6.37 us (17%)
  waiting for transfers between devices  6.36 us (17%)
  between operations  0.84 us (2%)
  loops' own time  0.4 us (1%)
    ppermute x8, starting transfers between devices, program(): direct.append(lax.ppermute(sent, 'col', around))  17.1 us
    ppermute x8, waiting for transfers between devices, program(): direct.append(lax.ppermute(sent, 'col', around))  5.76 us
    ppermute x2, starting transfers between devices, turn(): return lax.ppermute(array, ('row', 'col'), pairs)  4.58 us
    pallas_call x1, Pallas kernels, shards(): pl.pallas_call(functools.partial(prepare_kernel, rows, col_tiles, row_til...  1.89 us
    pallas_call x2, Pallas kernels, add_last(): pl.pallas_call(functools.partial(add_last_kernel, most, t), out_shape=res...  1.77 us
    pallas_call x1, Pallas kernels, program(): pl.pallas_call(early_product_kernel, out_shape=(partial,) * PARTS, in_spe...  1.25 us
  transfers between devices with their start and end apart: 20, of which 8 were waited for; matrix products, arithmetic and copies ran while one was open for 0% of the time, Pallas kernels for 10%

profile of v1, /device:TPU:0, one launch (start us, length us, event | category | flops | bytes accessed | tf_op | source)
XLA Modules:
  0.0 36.9 jit_solution(13208044174443832000)
XLA Ops:
  0.0 1.9 %prepare.1 = (bf16[512,512]{1,0:T(8,128)(2,1)S(1)}, bf16[512,512]{1,0:T(8,128)(2,1)S(1)}, s32[64,128]{1,0:T(8,128)S(1)}, s32[1]{0:T(128)}) custom-call(s32[4]{0:T(128)} %sections_in.1, s32[2,4]{1,0:T(2,128)} %bitcast.18, bf16[1024,512]{1,0:T(8,128)(2,1)} %values.1), custom_call_target="tpu_custom_call" | custom-call | tf_op jit(solution)/shard_map/prepare/pallas_call | solution.py:549
  2.5 34.2 %conditional.1 = (bf16[1024,512]{1,0:T(8,128)(2,1)}) conditional(s32[]{:T(128)} %bitcast.5, (bf16[512,512]{1,0:T(8,128)(2,1)S(1)}, bf16[512,512]{1,0:T(8,128)(2,1)S(1)}, s32[64,128]{1,0:T(8,128)S(1)}) %tuple.61, (bf16[512,512]{1,0:T(8,128)(2,1)S(1)}, bf16[512,512]{1,0:T(8,128)(2,1)S(1)}, ...), branch_computations={%region_0.0_spmd, %region_1.0_spmd, %region_2.0_spmd, %region_3.0_... | conditional | bytes 37749904 | solution.py:570
  2.6 0.5 %collective-permute-start.17 = (bf16[512,512]{1,0:T(8,128)(2,1)S(1)}, bf16[512,512]{1,0:T(8,128)(2,1)S(1)}, u32[]{:S(2)}, u32[]{:S(2)}) collective-permute-start(bf16[512,512]{1,0:T(8,128)(2,1)S(1)} %get-tuple-element.63.masked.refs_0_), channel_id=1, source_target_pairs={{0,1},{1,0},{2,3},{3,2},{4,5},{5,4},{6,7},{7,6},{8,9},{9,8},{10,11... | collective-permute-start | bytes 1572872 | tf_op jit(solution)/shard_map/cond/branch_1_fun/ppermute | solution.py:429
  3.1 0.1 collective-permute-start.16
  3.2 0.1 own_rows.5.refs_0_
  3.3 3.0 %collective-permute-start.20 = (bf16[2,256,512]{2,1,0:T(8,128)(2,1)S(1)}, bf16[2,256,512]{2,1,0:T(8,128)(2,1)S(1)}, u32[]{:S(2)}, u32[]{:S(2)}) collective-permute-start(bf16[2,256,512]{2,1,0:T(8,128)(2,1)S(1)} %own_rows.5.refs_0_), channel_id=1, source_target_pairs={{0,8},{1,17},{2,10},{3,19},{4,12},{5,21},{6,14},{7,23},{8,0},{9,25... | collective-permute-start | bytes 1572872 | tf_op jit(solution)/shard_map/cond/branch_1_fun/ppermute | solution.py:427
  6.3 1.5 %collective-permute-start.19 = (bf16[512,256]{1,0:T(8,128)(2,1)S(1)}, bf16[512,256]{1,0:T(8,128)(2,1)S(1)}, u32[]{:S(2)}, u32[]{:S(2)}) collective-permute-start(bf16[512,256]{1,0:T(8,128)(2,1)S(1)} %choose.42.refs_0_), channel_id=1, source_target_pairs={{0,2},{2,4},{4,6},{6,7},{7,5},{5,3},{3,1},{1,0},{8,10},{10,12},{12... | collective-permute-start | bytes 786440 | tf_op jit(solution)/shard_map/cond/branch_1_fun/ppermute | solution.py:476
  8.0 1.6 %collective-permute-start.18 = (bf16[512,256]{1,0:T(8,128)(2,1)S(1)}, bf16[512,256]{1,0:T(8,128)(2,1)S(1)}, u32[]{:S(2)}, u32[]{:S(2)}) collective-permute-start(bf16[512,256]{1,0:T(8,128)(2,1)S(1)} %choose.43.refs_1_), channel_id=1, source_target_pairs={{0,2},{2,4},{4,6},{6,7},{7,5},{5,3},{3,1},{1,0},{8,10},{10,12},{12... | collective-permute-start | bytes 786440 | tf_op jit(solution)/shard_map/cond/branch_1_fun/ppermute | solution.py:476
  9.6 2.2 %collective-permute-done.19.refs_0_.refs_4_ = bf16[512,256]{1,0:T(8,128)(2,1)S(1)} collective-permute-done((bf16[512,256]{1,0:T(8,128)(2,1)S(1)}, bf16[512,256]{1,0:T(8,128)(2,1)S(1)}, u32[]{:S(2)}, u32[]{:S(2)}) %collective-permute-start.19) | collective-permute-done | bytes 262176 | tf_op jit(solution)/shard_map/cond/branch_1_fun/ppermute | solution.py:476
  11.8 0.1 choose.44.refs_1_
  11.9 2.5 %collective-permute-start.22 = (bf16[512,256]{1,0:T(8,128)(2,1)S(1)}, bf16[512,256]{1,0:T(8,128)(2,1)S(1)}, u32[]{:S(2)}, u32[]{:S(2)}) collective-permute-start(bf16[512,256]{1,0:T(8,128)(2,1)S(1)} %choose.44.refs_1_), channel_id=1, source_target_pairs={{0,2},{2,4},{4,6},{6,7},{7,5},{5,3},{3,1},{1,0},{8,10},{10,12},{12... | collective-permute-start | bytes 786440 | tf_op jit(solution)/shard_map/cond/branch_1_fun/ppermute | solution.py:476
  14.4 0.2 collective-permute-done.18.refs_0_.refs_2_.refs_10_
  14.6 0.1 choose.45.refs_1_
  14.7 2.5 %collective-permute-start.21 = (bf16[512,256]{1,0:T(8,128)(2,1)S(1)}, bf16[512,256]{1,0:T(8,128)(2,1)S(1)}, u32[]{:S(2)}, u32[]{:S(2)}) collective-permute-start(bf16[512,256]{1,0:T(8,128)(2,1)S(1)} %choose.45.refs_1_), channel_id=1, source_target_pairs={{0,2},{2,4},{4,6},{6,7},{7,5},{5,3},{3,1},{1,0},{8,10},{10,12},{12... | collective-permute-start | bytes 786440 | tf_op jit(solution)/shard_map/cond/branch_1_fun/ppermute | solution.py:476
  17.2 0.1 near_rows.5.near
  17.3 1.6 %collective-permute-start.34 = (bf16[3,256,512]{2,1,0:T(8,128)(2,1)S(1)}, bf16[3,256,512]{2,1,0:T(8,128)(2,1)S(1)}, u32[]{:S(2)}, u32[]{:S(2)}) collective-permute-start(bf16[3,256,512]{2,1,0:T(8,128)(2,1)S(1)} %near_rows.5.near), channel_id=1, source_target_pairs={{0,16},{1,9},{2,18},{3,11},{4,20},{5,13},{6,22},{7,15},{8,24},{9,1... | collective-permute-start | bytes 2359304 | tf_op jit(solution)/shard_map/cond/branch_1_fun/ppermute | solution.py:427
  19.0 1.8 %collective-permute-start.26 = (bf16[512,256]{1,0:T(8,128)(2,1)S(1)}, bf16[512,256]{1,0:T(8,128)(2,1)S(1)}, u32[]{:S(2)}, u32[]{:S(2)}) collective-permute-start(bf16[512,256]{1,0:T(8,128)(2,1)S(1)} %choose.46.refs_1_), channel_id=1, source_target_pairs={{0,2},{2,4},{4,6},{6,7},{7,5},{5,3},{3,1},{1,0},{8,10},{10,12},{12... | collective-permute-start | bytes 786440 | tf_op jit(solution)/shard_map/cond/branch_1_fun/ppermute | solution.py:476
  20.8 0.2 collective-permute-done.21.refs_0_.refs_11_
  21.1 2.5 %collective-permute-start.25 = (bf16[512,256]{1,0:T(8,128)(2,1)S(1)}, bf16[512,256]{1,0:T(8,128)(2,1)S(1)}, u32[]{:S(2)}, u32[]{:S(2)}) collective-permute-start(bf16[512,256]{1,0:T(8,128)(2,1)S(1)} %choose.47.refs_1_), channel_id=1, source_target_pairs={{0,2},{2,4},{4,6},{6,7},{7,5},{5,3},{3,1},{1,0},{8,10},{10,12},{12... | collective-permute-start | bytes 786440 | tf_op jit(solution)/shard_map/cond/branch_1_fun/ppermute | solution.py:476
  23.6 1.1 %collective-permute-done.26.refs_0_.refs_6_ = bf16[512,256]{1,0:T(8,128)(2,1)S(1)} collective-permute-done((bf16[512,256]{1,0:T(8,128)(2,1)S(1)}, bf16[512,256]{1,0:T(8,128)(2,1)S(1)}, u32[]{:S(2)}, u32[]{:S(2)}) %collective-permute-start.26) | collective-permute-done | bytes 262176 | tf_op jit(solution)/shard_map/cond/branch_1_fun/ppermute | solution.py:476
  24.9 2.5 %collective-permute-start.30 = (bf16[512,256]{1,0:T(8,128)(2,1)S(1)}, bf16[512,256]{1,0:T(8,128)(2,1)S(1)}, u32[]{:S(2)}, u32[]{:S(2)}) collective-permute-start(bf16[512,256]{1,0:T(8,128)(2,1)S(1)} %choose.48.refs_1_), channel_id=1, source_target_pairs={{0,2},{2,4},{4,6},{6,7},{7,5},{5,3},{3,1},{1,0},{8,10},{10,12},{12... | collective-permute-start | bytes 786440 | tf_op jit(solution)/shard_map/cond/branch_1_fun/ppermute | solution.py:476
  27.4 0.1 collective-permute-done.25.refs_0_.refs_12_
  27.6 0.4 %collective-permute-start.33 = (bf16[512,256]{1,0:T(8,128)(2,1)S(1)}, bf16[512,256]{1,0:T(8,128)(2,1)S(1)}, u32[]{:S(2)}, u32[]{:S(2)}) collective-permute-start(bf16[512,256]{1,0:T(8,128)(2,1)S(1)} %collective-permute-done.25.refs_0_.refs_12_), channel_id=1, source_target_pairs={{0,1},{1,0},{2,3},{3,2},{4,5},{5,4},{6,7},{7,6},{8,9},{9,8},{10,11... | collective-permute-start | bytes 786440 | tf_op jit(solution)/shard_map/cond/branch_1_fun/ppermute | solution.py:475
  28.1 2.1 %collective-permute-start.29 = (bf16[512,256]{1,0:T(8,128)(2,1)S(1)}, bf16[512,256]{1,0:T(8,128)(2,1)S(1)}, u32[]{:S(2)}, u32[]{:S(2)}) collective-permute-start(bf16[512,256]{1,0:T(8,128)(2,1)S(1)} %choose.49.refs_16_), channel_id=1, source_target_pairs={{0,2},{2,4},{4,6},{6,7},{7,5},{5,3},{3,1},{1,0},{8,10},{10,12},{12... | collective-permute-start | bytes 786440 | tf_op jit(solution)/shard_map/cond/branch_1_fun/ppermute | solution.py:476
  30.2 1.1 %collective-permute-done.30.direct = bf16[512,256]{1,0:T(8,128)(2,1)S(1)} collective-permute-done((bf16[512,256]{1,0:T(8,128)(2,1)S(1)}, bf16[512,256]{1,0:T(8,128)(2,1)S(1)}, u32[]{:S(2)}, u32[]{:S(2)}) %collective-permute-start.30) | collective-permute-done | bytes 262176 | tf_op jit(solution)/shard_map/cond/branch_1_fun/ppermute | solution.py:476
  31.4 0.1 all_rows.5
  31.5 0.5 %gather.5 = (bf16[512,1024]{1,0:T(8,128)(2,1)S(1)}, bf16[512,1024]{1,0:T(8,128)(2,1)S(1)}) custom-call(s32[64,128]{1,0:T(8,128)S(1)} %get-tuple-element.61.table, bf16[512,512]{1,0:T(8,128)(2,1)S(1)} %get-tuple-element.63.masked.refs_0_, bf16[512,512]{1,0:T(8,128)(2,1)S(1)} %collective-permute-done.17.got.refs_1_, ...), custom_call_target="tpu_custom_call" | custom-call | tf_op jit(solution)/shard_map/cond/branch_1_fun/gather/pallas_call | solution.py:508
  32.0 1.2 %early_product.5 = (f32[512,512]{1,0:T(8,128)S(1)}, f32[512,512]{1,0:T(8,128)S(1)}) custom-call(bf16[512,1024]{1,0:T(8,128)(2,1)S(1)} %get-tuple-element.82.refs_0_, bf16[512,1024]{1,0:T(8,128)(2,1)S(1)} %get-tuple-element.83.refs_1_, bf16[1024,512]{1,0:T(8,128)(2,1)S(1)} %bitcast.15), custom_call_target="tpu_custom_call" | custom-call | tf_op jit(solution)/shard_map/cond/branch_1_fun/early_product/pallas_call | solution.py:517
  33.3 0.8 %collective-permute-done.29.direct = bf16[512,256]{1,0:T(8,128)(2,1)S(1)} collective-permute-done((bf16[512,256]{1,0:T(8,128)(2,1)S(1)}, bf16[512,256]{1,0:T(8,128)(2,1)S(1)}, u32[]{:S(2)}, u32[]{:S(2)}) %collective-permute-start.29) | collective-permute-done | bytes 262176 | tf_op jit(solution)/shard_map/cond/branch_1_fun/ppermute | solution.py:476
  34.2 0.9 %add_last.10.refs_0_ = bf16[1024,512]{1,0:T(8,128)(2,1)} custom-call(s32[64,128]{1,0:T(8,128)S(1)} %get-tuple-element.61.table, f32[512,512]{1,0:T(8,128)S(1)} %get-tuple-element.89.early, bf16[1024,512]{1,0:T(8,128)(2,1)S(1)} %bitcast.16, bf16[512,256]{1,0:T(8,128)(2,1)S(1)} %collective-permute-done.30.direct, ...), custom_call_target="tpu_custom_call" | custom-call | tf_op jit(solution)/shard_map/cond/branch_1_fun/add_last/pallas_call | solution.py:529
  35.1 0.6 %collective-permute-done.35.passed = bf16[512,256]{1,0:T(8,128)(2,1)S(1)} collective-permute-done((bf16[512,256]{1,0:T(8,128)(2,1)S(1)}, bf16[512,256]{1,0:T(8,128)(2,1)S(1)}, u32[]{:S(2)}, u32[]{:S(2)}) %collective-permute-start.35) | collective-permute-done | bytes 262176 | tf_op jit(solution)/shard_map/cond/branch_1_fun/ppermute | solution.py:526
  35.6 0.9 %add_last.11 = bf16[1024,512]{1,0:T(8,128)(2,1)} custom-call(s32[64,128]{1,0:T(8,128)S(1)} %get-tuple-element.61.table, f32[512,512]{1,0:T(8,128)S(1)} %get-tuple-element.87.early, bf16[1024,512]{1,0:T(8,128)(2,1)S(1)} %bitcast.17, bf16[512,256]{1,0:T(8,128)(2,1)S(1)} %collective-permute-done.29.direct, ...), custom_call_target="tpu_custom_call", output_to_operand_aliasing={{}: (5, {})} | custom-call | tf_op jit(solution)/shard_map/cond/branch_1_fun/add_last/pallas_call | solution.py:529
  (25 shorter events, 0.7 us)
Async XLA Ops:
  2.6 3.7 %collective-permute-start.17 = (bf16[512,512]{1,0:T(8,128)(2,1)S(1)}, bf16[512,512]{1,0:T(8,128)(2,1)S(1)}, u32[]{:S(2)}, u32[]{:S(2)}) collective-permute-start(bf16[512,512]{1,0:T(8,128)(2,1)S(1)} %get-tuple-element.63.masked.refs_0_), channel_id=1, source_target_pairs={{0,1},{1,0},{2,3},{3,2},{4,5},{5,4},{6,7},{7,6},{8,9},{9,8},{10,11... | collective-permute-start | bytes 1572872 | tf_op jit(solution)/shard_map/cond/branch_1_fun/ppermute | solution.py:429
  3.1 4.8 %collective-permute-start.16 = (bf16[512,512]{1,0:T(8,128)(2,1)S(1)}, bf16[512,512]{1,0:T(8,128)(2,1)S(1)}, u32[]{:S(2)}, u32[]{:S(2)}) collective-permute-start(bf16[512,512]{1,0:T(8,128)(2,1)S(1)} %get-tuple-element.62.masked.refs_1_.refs_2_), channel_id=1, source_target_pairs={{0,1},{1,0},{2,3},{3,2},{4,5},{5,4},{6,7},{7,6},{8,9},{9,8},{10,11... | collective-permute-start | bytes 1572872 | tf_op jit(solution)/shard_map/cond/branch_1_fun/ppermute | solution.py:429
  3.3 11.1 %collective-permute-start.20 = (bf16[2,256,512]{2,1,0:T(8,128)(2,1)S(1)}, bf16[2,256,512]{2,1,0:T(8,128)(2,1)S(1)}, u32[]{:S(2)}, u32[]{:S(2)}) collective-permute-start(bf16[2,256,512]{2,1,0:T(8,128)(2,1)S(1)} %own_rows.5.refs_0_), channel_id=1, source_target_pairs={{0,8},{1,17},{2,10},{3,19},{4,12},{5,21},{6,14},{7,23},{8,0},{9,25... | collective-permute-start | bytes 1572872 | tf_op jit(solution)/shard_map/cond/branch_1_fun/ppermute | solution.py:427
  6.3 5.4 %collective-permute-start.19 = (bf16[512,256]{1,0:T(8,128)(2,1)S(1)}, bf16[512,256]{1,0:T(8,128)(2,1)S(1)}, u32[]{:S(2)}, u32[]{:S(2)}) collective-permute-start(bf16[512,256]{1,0:T(8,128)(2,1)S(1)} %choose.42.refs_0_), channel_id=1, source_target_pairs={{0,2},{2,4},{4,6},{6,7},{7,5},{5,3},{3,1},{1,0},{8,10},{10,12},{12... | collective-permute-start | bytes 786440 | tf_op jit(solution)/shard_map/cond/branch_1_fun/ppermute | solution.py:476
  8.0 6.6 %collective-permute-start.18 = (bf16[512,256]{1,0:T(8,128)(2,1)S(1)}, bf16[512,256]{1,0:T(8,128)(2,1)S(1)}, u32[]{:S(2)}, u32[]{:S(2)}) collective-permute-start(bf16[512,256]{1,0:T(8,128)(2,1)S(1)} %choose.43.refs_1_), channel_id=1, source_target_pairs={{0,2},{2,4},{4,6},{6,7},{7,5},{5,3},{3,1},{1,0},{8,10},{10,12},{12... | collective-permute-start | bytes 786440 | tf_op jit(solution)/shard_map/cond/branch_1_fun/ppermute | solution.py:476
  11.9 7.0 %collective-permute-start.22 = (bf16[512,256]{1,0:T(8,128)(2,1)S(1)}, bf16[512,256]{1,0:T(8,128)(2,1)S(1)}, u32[]{:S(2)}, u32[]{:S(2)}) collective-permute-start(bf16[512,256]{1,0:T(8,128)(2,1)S(1)} %choose.44.refs_1_), channel_id=1, source_target_pairs={{0,2},{2,4},{4,6},{6,7},{7,5},{5,3},{3,1},{1,0},{8,10},{10,12},{12... | collective-permute-start | bytes 786440 | tf_op jit(solution)/shard_map/cond/branch_1_fun/ppermute | solution.py:476
  14.4 4.5 %collective-permute-start.23 = (bf16[512,256]{1,0:T(8,128)(2,1)S(1)}, bf16[512,256]{1,0:T(8,128)(2,1)S(1)}, u32[]{:S(2)}, u32[]{:S(2)}) collective-permute-start(bf16[512,256]{1,0:T(8,128)(2,1)S(1)} %collective-permute-done.19.refs_0_.refs_4_), channel_id=1, source_target_pairs={{0,1},{1,0},{2,3},{3,2},{4,5},{5,4},{6,7},{7,6},{8,9},{9,8},{10,11... | collective-permute-start | bytes 786440 | tf_op jit(solution)/shard_map/cond/branch_1_fun/ppermute | solution.py:475
  14.7 6.4 %collective-permute-start.21 = (bf16[512,256]{1,0:T(8,128)(2,1)S(1)}, bf16[512,256]{1,0:T(8,128)(2,1)S(1)}, u32[]{:S(2)}, u32[]{:S(2)}) collective-permute-start(bf16[512,256]{1,0:T(8,128)(2,1)S(1)} %choose.45.refs_1_), channel_id=1, source_target_pairs={{0,2},{2,4},{4,6},{6,7},{7,5},{5,3},{3,1},{1,0},{8,10},{10,12},{12... | collective-permute-start | bytes 786440 | tf_op jit(solution)/shard_map/cond/branch_1_fun/ppermute | solution.py:476
  17.2 3.9 %collective-permute-start.24 = (bf16[512,256]{1,0:T(8,128)(2,1)S(1)}, bf16[512,256]{1,0:T(8,128)(2,1)S(1)}, u32[]{:S(2)}, u32[]{:S(2)}) collective-permute-start(bf16[512,256]{1,0:T(8,128)(2,1)S(1)} %collective-permute-done.18.refs_0_.refs_2_.refs_10_), channel_id=1, source_target_pairs={{0,1},{1,0},{2,3},{3,2},{4,5},{5,4},{6,7},{7,6},{8,9},{9,8},{10,11... | collective-permute-start | bytes 786440 | tf_op jit(solution)/shard_map/cond/branch_1_fun/ppermute | solution.py:475
  17.3 14.1 %collective-permute-start.34 = (bf16[3,256,512]{2,1,0:T(8,128)(2,1)S(1)}, bf16[3,256,512]{2,1,0:T(8,128)(2,1)S(1)}, u32[]{:S(2)}, u32[]{:S(2)}) collective-permute-start(bf16[3,256,512]{2,1,0:T(8,128)(2,1)S(1)} %near_rows.5.near), channel_id=1, source_target_pairs={{0,16},{1,9},{2,18},{3,11},{4,20},{5,13},{6,22},{7,15},{8,24},{9,1... | collective-permute-start | bytes 2359304 | tf_op jit(solution)/shard_map/cond/branch_1_fun/ppermute | solution.py:427
  19.0 5.7 %collective-permute-start.26 = (bf16[512,256]{1,0:T(8,128)(2,1)S(1)}, bf16[512,256]{1,0:T(8,128)(2,1)S(1)}, u32[]{:S(2)}, u32[]{:S(2)}) collective-permute-start(bf16[512,256]{1,0:T(8,128)(2,1)S(1)} %choose.46.refs_1_), channel_id=1, source_target_pairs={{0,2},{2,4},{4,6},{6,7},{7,5},{5,3},{3,1},{1,0},{8,10},{10,12},{12... | collective-permute-start | bytes 786440 | tf_op jit(solution)/shard_map/cond/branch_1_fun/ppermute | solution.py:476
  20.8 3.9 %collective-permute-start.27 = (bf16[512,256]{1,0:T(8,128)(2,1)S(1)}, bf16[512,256]{1,0:T(8,128)(2,1)S(1)}, u32[]{:S(2)}, u32[]{:S(2)}) collective-permute-start(bf16[512,256]{1,0:T(8,128)(2,1)S(1)} %collective-permute-done.22.refs_0_.refs_5_), channel_id=1, source_target_pairs={{0,1},{1,0},{2,3},{3,2},{4,5},{5,4},{6,7},{7,6},{8,9},{9,8},{10,11... | collective-permute-start | bytes 786440 | tf_op jit(solution)/shard_map/cond/branch_1_fun/ppermute | solution.py:475
  21.1 6.4 %collective-permute-start.25 = (bf16[512,256]{1,0:T(8,128)(2,1)S(1)}, bf16[512,256]{1,0:T(8,128)(2,1)S(1)}, u32[]{:S(2)}, u32[]{:S(2)}) collective-permute-start(bf16[512,256]{1,0:T(8,128)(2,1)S(1)} %choose.47.refs_1_), channel_id=1, source_target_pairs={{0,2},{2,4},{4,6},{6,7},{7,5},{5,3},{3,1},{1,0},{8,10},{10,12},{12... | collective-permute-start | bytes 786440 | tf_op jit(solution)/shard_map/cond/branch_1_fun/ppermute | solution.py:476
  24.8 2.7 %collective-permute-start.28 = (bf16[512,256]{1,0:T(8,128)(2,1)S(1)}, bf16[512,256]{1,0:T(8,128)(2,1)S(1)}, u32[]{:S(2)}, u32[]{:S(2)}) collective-permute-start(bf16[512,256]{1,0:T(8,128)(2,1)S(1)} %collective-permute-done.26.refs_0_.refs_6_), channel_id=1, source_target_pairs={{0,1},{1,0},{2,3},{3,2},{4,5},{5,4},{6,7},{7,6},{8,9},{9,8},{10,11... | collective-permute-start | bytes 786440 | tf_op jit(solution)/shard_map/cond/branch_1_fun/ppermute | solution.py:475
  24.9 6.4 %collective-permute-start.30 = (bf16[512,256]{1,0:T(8,128)(2,1)S(1)}, bf16[512,256]{1,0:T(8,128)(2,1)S(1)}, u32[]{:S(2)}, u32[]{:S(2)}) collective-permute-start(bf16[512,256]{1,0:T(8,128)(2,1)S(1)} %choose.48.refs_1_), channel_id=1, source_target_pairs={{0,2},{2,4},{4,6},{6,7},{7,5},{5,3},{3,1},{1,0},{8,10},{10,12},{12... | collective-permute-start | bytes 786440 | tf_op jit(solution)/shard_map/cond/branch_1_fun/ppermute | solution.py:476
  27.4 4.1 %collective-permute-start.32 = (bf16[512,256]{1,0:T(8,128)(2,1)S(1)}, bf16[512,256]{1,0:T(8,128)(2,1)S(1)}, u32[]{:S(2)}, u32[]{:S(2)}) collective-permute-start(bf16[512,256]{1,0:T(8,128)(2,1)S(1)} %collective-permute-done.21.refs_0_.refs_11_), channel_id=1, source_target_pairs={{0,1},{1,0},{2,3},{3,2},{4,5},{5,4},{6,7},{7,6},{8,9},{9,8},{10,11... | collective-permute-start | bytes 786440 | tf_op jit(solution)/shard_map/cond/branch_1_fun/ppermute | solution.py:475
  27.6 3.9 %collective-permute-start.33 = (bf16[512,256]{1,0:T(8,128)(2,1)S(1)}, bf16[512,256]{1,0:T(8,128)(2,1)S(1)}, u32[]{:S(2)}, u32[]{:S(2)}) collective-permute-start(bf16[512,256]{1,0:T(8,128)(2,1)S(1)} %collective-permute-done.25.refs_0_.refs_12_), channel_id=1, source_target_pairs={{0,1},{1,0},{2,3},{3,2},{4,5},{5,4},{6,7},{7,6},{8,9},{9,8},{10,11... | collective-permute-start | bytes 786440 | tf_op jit(solution)/shard_map/cond/branch_1_fun/ppermute | solution.py:475
  28.1 6.0 %collective-permute-start.29 = (bf16[512,256]{1,0:T(8,128)(2,1)S(1)}, bf16[512,256]{1,0:T(8,128)(2,1)S(1)}, u32[]{:S(2)}, u32[]{:S(2)}) collective-permute-start(bf16[512,256]{1,0:T(8,128)(2,1)S(1)} %choose.49.refs_16_), channel_id=1, source_target_pairs={{0,2},{2,4},{4,6},{6,7},{7,5},{5,3},{3,1},{1,0},{8,10},{10,12},{12... | collective-permute-start | bytes 786440 | tf_op jit(solution)/shard_map/cond/branch_1_fun/ppermute | solution.py:476
  31.3 2.8 %collective-permute-start.31 = (bf16[512,256]{1,0:T(8,128)(2,1)S(1)}, bf16[512,256]{1,0:T(8,128)(2,1)S(1)}, u32[]{:S(2)}, u32[]{:S(2)}) collective-permute-start(bf16[512,256]{1,0:T(8,128)(2,1)S(1)} %collective-permute-done.30.direct), channel_id=1, source_target_pairs={{0,1},{1,0},{2,3},{3,2},{4,5},{5,4},{6,7},{7,6},{8,9},{9,8},{10,11... | collective-permute-start | bytes 786440 | tf_op jit(solution)/shard_map/cond/branch_1_fun/ppermute | solution.py:477
  34.1 1.5 %collective-permute-start.35 = (bf16[512,256]{1,0:T(8,128)(2,1)S(1)}, bf16[512,256]{1,0:T(8,128)(2,1)S(1)}, u32[]{:S(2)}, u32[]{:S(2)}) collective-permute-start(bf16[512,256]{1,0:T(8,128)(2,1)S(1)} %collective-permute-done.29.direct), channel_id=1, source_target_pairs={{0,1},{1,0},{2,3},{3,2},{4,5},{5,4},{6,7},{7,6},{8,9},{9,8},{10,11... | collective-permute-start | bytes 786440 | tf_op jit(solution)/shard_map/cond/branch_1_fun/ppermute | solution.py:526
